TPU v7x, 32 devices: a whole 2x2x4 slice. The times are simulated.
32 devices in a mesh: tile: 16 (over z, x, core), mode: 2 (over y).
Axes of the slice: x: 2, y: 2, z: 4, core: 2. Of those that a mesh axis runs over, the one named last changes fastest.
Arguments:
- object_field: float32 [2, 4096, 1024], P(None, 'tile'), may hold values from -6 to 6
- probe_modes: float32 [2, 8, 256, 256], P(None, 'mode'), may hold values from -1.5 to 1.5
- measured: float32 [128, 256, 256], P('tile'), may hold values from 0.05 to 4
- row_starts: int32 [128], P('tile'), may hold values from -128 to 128, as said below
- col_starts: int32 [128], P('tile'), may hold values from 0 to 768
- live_counts: int32 [16], P('tile'), may hold values from 1 to 8, 96 in all
Outputs:
- object_grad: float32 [2, 4096, 1024], P(None, 'tile', 'mode')
- probe_grad: float32 [2, 8, 256, 256], P(None, 'mode')
Inputs may be any that keep to these rules, and one draw needn't show every extreme that they name: A window lies inside the object: on tile 0 row_starts is at least 0, on the last tile at most 0; elsewhere a window reaches at most 128 rows into the tile above or below. `live_counts`: slots of a tile from its count on are unused.
All inputs are finite; a program needn't handle non-finite values. No bound on the sum of `live_counts` on one device may be relied on, other than what follows from the above.
Results may differ from a plain program's by a relative error of at most 0.0056.
Values sent between devices are 32-bit elements; how exact they have to be, the bound alone decides.
A program may use at most 128 MiB of HBM per device.

v0:
```python
import math

import jax
import jax.numpy as jnp
from jax import lax
from jax.sharding import PartitionSpec as P


def padded_2(value, sides, width):
    for axis, dim in sides:
        peers, length = (lax.axis_size(axis), value.shape[dim])
        up = [(i, (i + 1) % peers) for i in range(peers - 1)]
        down = [(j, i) for i, j in up]
        last = lax.slice_in_dim(value, length - width, length, axis=dim)
        leading = lax.slice_in_dim(value, 0, width, axis=dim)
        before = lax.ppermute(last, axis, up)
        after = lax.ppermute(leading, axis, down)
        value = jnp.concatenate([before, value, after], axis=dim)
    return value


def passed_along(value, axis, steps):
    count = lax.axis_size(axis)
    leading, last = (max(0, -steps), min(count, count - steps))
    return lax.ppermute(value, axis, [(source, source + steps) for source in range(leading, last)])


def dft_blocks(window, conj_sign):
    index_range = jnp.arange(window, dtype=jnp.int32)
    phases = index_range[:, None] * index_range[None, :] % window
    angles = phases.astype(jnp.float32) * (-2.0 * math.pi / window)
    norm_scale = 1.0 / math.sqrt(window)
    cosine_table = (jnp.cos(angles) * norm_scale).astype(jnp.bfloat16)
    sine_table = (jnp.sin(angles) * (norm_scale * conj_sign)).astype(jnp.bfloat16)
    return jnp.stack(
        [jnp.stack([cosine_table, -sine_table]), jnp.stack([sine_table, cosine_table])]
    )


def transform(wave_field, blocks_table):
    half_pass = jnp.einsum(
        "abkr,bpmrc->apmkc", blocks_table, wave_field, preferred_element_type=jnp.float32
    ).astype(jnp.bfloat16)
    return jnp.einsum(
        "bpmrc,abck->apmrk", half_pass, blocks_table, preferred_element_type=jnp.float32
    )


def complex_times(left_factor, right_factor):
    return jnp.stack(
        [
            left_factor[0] * right_factor[0] - left_factor[1] * right_factor[1],
            left_factor[0] * right_factor[1] + left_factor[1] * right_factor[0],
        ]
    )


def conj_times(left_factor, right_factor):
    return jnp.stack(
        [
            left_factor[0] * right_factor[0] + left_factor[1] * right_factor[1],
            left_factor[0] * right_factor[1] - left_factor[1] * right_factor[0],
        ]
    )


def amplitude_scaling(model_intensity, measured_block, live_block):
    floored = jnp.maximum(jnp.sqrt(model_intensity), 0.5)
    return live_block[:, None, None] * (1.0 - jnp.sqrt(measured_block) / floored)


def place_terms(accumulated, terms, row_tops, col_lefts):
    window = terms.shape[-1]
    zero_index = jnp.zeros((), jnp.int32)

    def place_one(position, current):
        anchor = (zero_index, row_tops[position], col_lefts[position])
        old_values = lax.dynamic_slice(current, anchor, (2, window, window))
        return lax.dynamic_update_slice(current, old_values + terms[:, position], anchor)

    return lax.fori_loop(0, terms.shape[1], place_one, accumulated)


def body(object_field, probe_modes, measured, row_starts, col_starts, live_counts):
    window = probe_modes.shape[-1]
    half_window = window // 2
    slot_count = row_starts.shape[0]
    tile_rows = object_field.shape[1]
    forward_blocks = dft_blocks(window, 1.0)
    backward_blocks = dft_blocks(window, -1.0)
    padded = padded_2(object_field, (("tile", 1),), half_window)
    row_tops = row_starts + half_window

    def take_patch(row_top, col_left):
        zero_index = jnp.zeros((), jnp.int32)
        return lax.dynamic_slice(padded, (zero_index, row_top, col_left), (2, window, window))

    patches = jax.vmap(take_patch, in_axes=(0, 0), out_axes=1)(row_tops, col_starts)
    live_mask = (jnp.arange(slot_count, dtype=jnp.int32) < live_counts[0]).astype(jnp.float32)
    exit_wave = complex_times(probe_modes[:, None], patches[:, :, None]).astype(jnp.bfloat16)
    far_field = transform(exit_wave, forward_blocks)
    partial_intensity = jnp.sum(far_field[0] * far_field[0] + far_field[1] * far_field[1], axis=1)
    model_intensity = lax.psum(partial_intensity, "mode")
    scaling = amplitude_scaling(model_intensity, measured, live_mask)
    residual_wave = (far_field * scaling[None, :, None]).astype(jnp.bfloat16)
    back_wave = transform(residual_wave, backward_blocks)
    object_terms = jnp.sum(conj_times(probe_modes[:, None], back_wave), axis=2)
    probe_terms = jnp.sum(conj_times(patches[:, :, None], back_wave), axis=1)
    probe_grad = lax.psum(probe_terms, "tile")
    buffer = place_terms(jnp.zeros(padded.shape, jnp.float32), object_terms, row_tops, col_starts)
    low_rim = buffer[:, :half_window]
    high_rim = buffer[:, tile_rows + half_window :]
    interior = buffer[:, half_window : half_window + tile_rows]
    from_next = passed_along(low_rim, "tile", -1)
    from_prev = passed_along(high_rim, "tile", 1)
    interior = interior.at[:, :half_window].add(from_prev)
    interior = interior.at[:, tile_rows - half_window :].add(from_next)
    object_grad = lax.psum_scatter(interior, "mode", scatter_dimension=2, tiled=True)
    return (object_grad, probe_grad)


def solution(mesh):
    return jax.shard_map(
        body,
        mesh=mesh,
        in_specs=(
            P(None, "tile", None),
            P(None, "mode", None, None),
            P("tile", None, None),
            P("tile"),
            P("tile"),
            P("tile"),
        ),
        out_specs=(P(None, "tile", "mode"), P(None, "mode", None, None)),
        check_vma=False,
    )
```

profile of v0, /device:TPU:0, one launch (start us, length us, event | category | flops | bytes accessed | tf_op | source)
XLA Modules:
  0.0 500.5 jit_solution(8209911999355078515)
XLA Ops:
  25.0 4.0 pad_maximum_fusion
  29.0 32.4 %while.17 = (s32[]{:T(128)}, f32[2,512,1024]{2,1,0:T(8,128)}, s32[8,3]{0,1:T(4,128)S(1)}, f32[8,2,256,256]{3,2,1,0:T(8,128)}, s32[]{:T(128)}) while((s32[]{:T(128)}, f32[2,512,1024]{2,1,0:T(8,128)}, s32[8,3]{0,1:T(4,128)S(1)}, f32[8,2,256,256]{3,2,1,0:T(8,128)}, s32[]{:T(128)}) %tuple.71), condition=%wide.while_cond.2, body=%wide.while_body.2.sunk | while | flops 2 | bytes 1050217 | solution.py:96
  29.6 3.5 bitcast_dynamic-update-slice_fusion.2
  33.6 3.4 bitcast_dynamic-update-slice_fusion.2
  37.6 3.5 bitcast_dynamic-update-slice_fusion.2
  41.7 3.5 bitcast_dynamic-update-slice_fusion.2
  45.7 3.5 bitcast_dynamic-update-slice_fusion.2
  49.8 3.4 bitcast_dynamic-update-slice_fusion.2
  53.8 3.4 bitcast_dynamic-update-slice_fusion.2
  57.8 3.5 bitcast_dynamic-update-slice_fusion.2
  61.3 4.6 slice_bitcast_fusion.1
  70.8 5.7 %subtract_convert_fusion = (bf16[1,8,4,256,256]{3,4,2,1,0:T(8,128)(2,1)}, bf16[1,8,4,256,256]{3,4,2,1,0:T(8,128)(2,1)}) fusion(f32[8,256,256]{1,2,0:T(8,128)} %copy.16, f32[4,256,256]{1,2,0:T(8,128)} %copy.15, f32[8,256,256]{1,2,0:T(8,128)S(1)} %copy.14, f32[4,256,256]{1,2,0:T(8,128)S(1)} %copy.13), kind=kLoop, calls=%fused_computation.26 | loop fusion | flops 16777216 | bytes 14680064 | tf_op jit(solution)/shard_map/convert
  76.5 15.8 %fusion.9 = f32[2,8,4,256,256]{3,4,2,1,0:T(8,128)} fusion(bf16[1,2,256,256]{2,3,1,0:T(8,128)(2,1)} %get-tuple-element.173, bf16[1,2,256,256]{2,3,1,0:T(8,128)(2,1)} %get-tuple-element.174, bf16[1,8,4,256,256]{3,4,2,1,0:T(8,128)(2,1)} %get-tuple-element.163, bf16[1,8,4,256,256]{3,4,2,1,0:T(8,128)(2,1)} %get-tuple-element.162), kind=kOutput, calls=%fused_computation.27 | convolution fusion | flops 8600420352 | bytes 25690112 | tf_op jit(solution)/shard_map/bpmrc,abck->apmrk/dot_general | solution.py:44
  92.3 8.2 %fusion.2 = f32[8,256,256]{1,2,0:T(8,128)} fusion(f32[2,8,4,256,256]{3,4,2,1,0:T(8,128)} %fusion.9), kind=kLoop, calls=%fused_computation.12 | loop fusion | flops 7864320 | bytes 18874368 | tf_op jit(solution)/shard_map/reduce_sum | solution.py:102
  104.3 74.5 %all-reduce.3.cloned.1.call-done = f32[8,256,256]{1,2,0:T(8,128)} async-done(((f32[8,256,256]{1,2,0:T(8,128)}), f32[8,256,256]{1,2,0:T(8,128)}) %all-reduce.3.cloned.1.call-update) | async-done | bytes 2097168 | tf_op jit(solution)/shard_map/psum | solution.py:103
  178.9 4.8 subtract_multiply_fusion
  183.7 18.9 %fusion.12 = f32[2,8,4,256,256]{3,4,2,1,0:T(8,128)} fusion(bf16[1,2,256,256]{2,3,1,0:T(8,128)(2,1)} %get-tuple-element.175, bf16[1,2,256,256]{2,3,1,0:T(8,128)(2,1)S(1)} %get-tuple-element.172, f32[2,8,4,256,256]{3,4,2,1,0:T(8,128)} %fusion.9, f32[8,256,256]{1,2,0:T(8,128)} %subtract_multiply_fusion), kind=kOutput, calls=%fused_computation.28 | convolution fusion | flops 8604614656 | bytes 36175872 | tf_op jit(solution)/shard_map/bpmrc,abck->apmrk/dot_general | solution.py:44
  202.6 17.7 %multiply_add_fusion = (f32[1,8,4,256,256]{3,4,2,1,0:T(8,128)}, f32[1,8,4,256,256]{3,4,2,1,0:T(8,128)}, f32[1,8,4,256,256]{3,4,2,1,0:T(8,128)}, f32[1,8,4,256,256]{3,4,2,1,0:T(8,128)}) fusion(f32[2,8,4,256,256]{3,4,2,1,0:T(8,128)} %fusion.12, f32[8,256,256]{1,2,0:T(8,128)} %copy.16, f32[8,256,256]{1,2,0:T(8,128)S(1)} %copy.14, f32[4,256,256]{1,2,0:T(8,128)} %copy.15, ...), kind=kLoop, calls=%fused_computation.22 | loop fusion | flops 25165824 | bytes 56623104 | tf_op jit(solution)/shard_map/add | solution.py:61
  220.3 9.7 %maximum_reduce_fusion = f32[2,8,256,256]{2,3,1,0:T(8,128)} fusion(f32[1,8,4,256,256]{3,4,2,1,0:T(8,128)} %get-tuple-element.160, f32[1,8,4,256,256]{3,4,2,1,0:T(8,128)} %get-tuple-element.161), kind=kLoop, calls=%fused_computation.4 | loop fusion | flops 7340032 | bytes 20971520 | tf_op jit(solution)/shard_map/reduce_sum | solution.py:107
  232.5 110.0 %while.16 = (s32[]{:T(128)}, f32[2,512,1024]{2,1,0:T(8,128)}, s32[8]{0:T(128)S(1)}, s32[8]{0:T(128)S(1)}, f32[2,8,256,256]{2,3,1,0:T(8,128)}, /*index=5*/s32[]{:T(128)}, s32[]{:T(128)}, s32[]{:T(128)}, s32[]{:T(128)}) while((s32[]{:T(128)}, f32[2,512,1024]{2,1,0:T(8,128)}, s32[8]{0:T(128)S(1)}, s32[8]{0:T(128)S(1)}, ...), condition=%wide.region_4.5_spmd, body=%wide.region_3.4_spmd.sunk | while | flops 131080 | bytes 4718793 | solution.py:81
  240.2 5.8 %dynamic_update_slice.8 = f32[2,512,1024]{2,1,0:T(8,128)} dynamic-update-slice(f32[2,512,1024]{2,1,0:T(8,128)} %get-tuple-element.267, f32[2,256,256]{2,1,0:T(8,128)S(1)} %bitcast_add_fusion.2, s32[]{:T(128)} %constant.116.clone.1..sunk, s32[]{:T(128)S(6)} %select_n.103, s32[]{:T(128)S(6)} %select_n.104) | dynamic-update-slice | bytes 1048580 | tf_op jit(solution)/shard_map/while/body/eval_jaxpr/dynamic_update_slice | solution.py:79
  253.6 4.6 dynamic_update_slice.8
  266.0 6.5 %dynamic_update_slice.8 = f32[2,512,1024]{2,1,0:T(8,128)} dynamic-update-slice(f32[2,512,1024]{2,1,0:T(8,128)} %get-tuple-element.267, f32[2,256,256]{2,1,0:T(8,128)S(1)} %bitcast_add_fusion.2, s32[]{:T(128)} %constant.116.clone.1..sunk, s32[]{:T(128)S(6)} %select_n.103, s32[]{:T(128)S(6)} %select_n.104) | dynamic-update-slice | bytes 1048580 | tf_op jit(solution)/shard_map/while/body/eval_jaxpr/dynamic_update_slice | solution.py:79
  280.3 5.8 %dynamic_update_slice.8 = f32[2,512,1024]{2,1,0:T(8,128)} dynamic-update-slice(f32[2,512,1024]{2,1,0:T(8,128)} %get-tuple-element.267, f32[2,256,256]{2,1,0:T(8,128)S(1)} %bitcast_add_fusion.2, s32[]{:T(128)} %constant.116.clone.1..sunk, s32[]{:T(128)S(6)} %select_n.103, s32[]{:T(128)S(6)} %select_n.104) | dynamic-update-slice | bytes 1048580 | tf_op jit(solution)/shard_map/while/body/eval_jaxpr/dynamic_update_slice | solution.py:79
  293.8 6.5 %dynamic_update_slice.8 = f32[2,512,1024]{2,1,0:T(8,128)} dynamic-update-slice(f32[2,512,1024]{2,1,0:T(8,128)} %get-tuple-element.267, f32[2,256,256]{2,1,0:T(8,128)S(1)} %bitcast_add_fusion.2, s32[]{:T(128)} %constant.116.clone.1..sunk, s32[]{:T(128)S(6)} %select_n.103, s32[]{:T(128)S(6)} %select_n.104) | dynamic-update-slice | bytes 1048580 | tf_op jit(solution)/shard_map/while/body/eval_jaxpr/dynamic_update_slice | solution.py:79
  308.1 6.2 %dynamic_update_slice.8 = f32[2,512,1024]{2,1,0:T(8,128)} dynamic-update-slice(f32[2,512,1024]{2,1,0:T(8,128)} %get-tuple-element.267, f32[2,256,256]{2,1,0:T(8,128)S(1)} %bitcast_add_fusion.2, s32[]{:T(128)} %constant.116.clone.1..sunk, s32[]{:T(128)S(6)} %select_n.103, s32[]{:T(128)S(6)} %select_n.104) | dynamic-update-slice | bytes 1048580 | tf_op jit(solution)/shard_map/while/body/eval_jaxpr/dynamic_update_slice | solution.py:79
  321.9 6.5 %dynamic_update_slice.8 = f32[2,512,1024]{2,1,0:T(8,128)} dynamic-update-slice(f32[2,512,1024]{2,1,0:T(8,128)} %get-tuple-element.267, f32[2,256,256]{2,1,0:T(8,128)S(1)} %bitcast_add_fusion.2, s32[]{:T(128)} %constant.116.clone.1..sunk, s32[]{:T(128)S(6)} %select_n.103, s32[]{:T(128)S(6)} %select_n.104) | dynamic-update-slice | bytes 1048580 | tf_op jit(solution)/shard_map/while/body/eval_jaxpr/dynamic_update_slice | solution.py:79
  336.2 6.3 %dynamic_update_slice.8 = f32[2,512,1024]{2,1,0:T(8,128)} dynamic-update-slice(f32[2,512,1024]{2,1,0:T(8,128)} %get-tuple-element.267, f32[2,256,256]{2,1,0:T(8,128)S(1)} %bitcast_add_fusion.2, s32[]{:T(128)} %constant.116.clone.1..sunk, s32[]{:T(128)S(6)} %select_n.103, s32[]{:T(128)S(6)} %select_n.104) | dynamic-update-slice | bytes 1048580 | tf_op jit(solution)/shard_map/while/body/eval_jaxpr/dynamic_update_slice | solution.py:79
  345.6 3.4 collective-permute-start.2
  350.3 8.5 %maximum_reduce_fusion.1 = f32[2,4,256,256]{2,3,1,0:T(8,128)} fusion(f32[1,8,4,256,256]{3,4,2,1,0:T(8,128)} %get-tuple-element.157, f32[1,8,4,256,256]{3,4,2,1,0:T(8,128)} %get-tuple-element.156), kind=kLoop, calls=%fused_computation.5 | loop fusion | flops 7864320 | bytes 18874368 | tf_op jit(solution)/shard_map/reduce_sum | solution.py:108
  363.9 96.2 %all-reduce.5.cloned.1.call-done = f32[2,4,256,256]{2,3,1,0:T(8,128)} async-done(((f32[2,4,256,256]{2,3,1,0:T(8,128)}), f32[2,4,256,256]{2,3,1,0:T(8,128)}) %all-reduce.5.cloned.1.call-update) | async-done | bytes 2097168 | tf_op jit(solution)/shard_map/psum | solution.py:109
  462.9 31.1 %reduce-scatter.2.cloned.1.call-done = f32[2,256,512]{2,1,0:T(8,128)} async-done(((f32[2,256,1024]{2,1,0:T(8,128)}), f32[2,256,512]{2,1,0:T(8,128)}) %reduce-scatter.2.cloned.1.call-update) | async-done | bytes 1048592 | tf_op jit(solution)/shard_map/reduce_scatter | solution.py:118
  (102 shorter events, 75.8 us)
Async XLA Ops:
  7.2 8.9 %copy-start.2 = (f32[2,4,256,256]{3,2,1,0:T(8,128)S(1)}, f32[2,4,256,256]{3,2,1,0:T(8,128)}, u32[]{:S(2)}) copy-start(f32[2,4,256,256]{3,2,1,0:T(8,128)} %param.13) | copy-start | bytes 6291460
  7.2 171.7 %all-reduce.3.cloned.1.call-start = ((), (), s32[]{:S(2)}) async-start(), calls=%async_computation.1 | async-start | bytes 4194304 | tf_op jit(solution)/shard_map/psum | solution.py:103
  10.5 14.5 %collective-permute-start = (f32[2,128,1024]{2,1,0:T(8,128)}, f32[2,128,1024]{2,1,0:T(8,128)}, u32[]{:S(2)}, u32[]{:S(2)}) collective-permute-start(f32[2,128,1024]{2,1,0:T(8,128)} %get-tuple-element.170), channel_id=1, source_target_pairs={{0,2},{2,4},{4,6},{6,8},{8,10},{10,12},{12,14},{14,16},{16,18},{18... | collective-permute-start | bytes 3145736 | tf_op jit(solution)/shard_map/ppermute | solution.py:16
  13.8 11.2 %collective-permute-start.1 = (f32[2,128,1024]{2,1,0:T(8,128)}, f32[2,128,1024]{2,1,0:T(8,128)}, u32[]{:S(2)}, u32[]{:S(2)}) collective-permute-start(f32[2,128,1024]{2,1,0:T(8,128)} %get-tuple-element.171), channel_id=1, source_target_pairs={{2,0},{4,2},{6,4},{8,6},{10,8},{12,10},{14,12},{16,14},{18,16},{20... | collective-permute-start | bytes 3145736 | tf_op jit(solution)/shard_map/ppermute | solution.py:17
  17.6 7.2 %copy-start.3 = (s32[8]{0:T(128)S(1)}, s32[8]{0:T(128)}, u32[]{:S(2)}) copy-start(s32[8]{0:T(128)} %param.15) | copy-start | bytes 100
  17.6 7.2 %copy-start.4 = (s32[8]{0:T(128)S(1)}, s32[8]{0:T(128)}, u32[]{:S(2)}) copy-start(s32[8]{0:T(128)} %param.16) | copy-start | bytes 100
  17.6 7.3 %copy-start.1 = (f32[2,256,1024]{2,1,0:T(8,128)S(1)}, f32[2,256,1024]{2,1,0:T(8,128)}, u32[]{:S(2)}) copy-start(f32[2,256,1024]{2,1,0:T(8,128)} %param.12) | copy-start | bytes 6291460
  100.5 359.5 %all-reduce.5.cloned.1.call-start = ((), (), s32[]{:S(2)}) async-start(), calls=%async_computation.3 | async-start | bytes 4194304 | tf_op jit(solution)/shard_map/psum | solution.py:109
  345.6 15.0 %collective-permute-start.2 = (f32[2,128,1024]{2,1,0:T(8,128)}, f32[2,128,1024]{2,1,0:T(8,128)}, u32[]{:S(2)}, u32[]{:S(2)}) collective-permute-start(f32[2,128,1024]{2,1,0:T(8,128)} %get-tuple-element.165), channel_id=1, source_target_pairs={{0,2},{2,4},{4,6},{6,8},{8,10},{10,12},{12,14},{14,16},{16,18},{18... | collective-permute-start | bytes 3145736 | tf_op jit(solution)/shard_map/ppermute | solution.py:25
  349.0 13.3 %collective-permute-start.3 = (f32[2,128,1024]{2,1,0:T(8,128)}, f32[2,128,1024]{2,1,0:T(8,128)S(1)}, u32[]{:S(2)}, u32[]{:S(2)}) collective-permute-start(f32[2,128,1024]{2,1,0:T(8,128)} %get-tuple-element.164), channel_id=1, source_target_pairs={{2,0},{4,2},{6,4},{8,6},{10,8},{12,10},{14,12},{16,14},{18,16},{20... | collective-permute-start | bytes 3145736 | tf_op jit(solution)/shard_map/ppermute | solution.py:25
  358.8 135.2 %reduce-scatter.2.cloned.1.call-start = ((), (), s32[]{:S(2)}) async-start(), calls=%async_computation.2 | async-start | bytes 3145728 | tf_op jit(solution)/shard_map/reduce_scatter | solution.py:118
  362.6 1.3 copy-start
Sparse Core Ops, SparseCore 0:
  100.6 78.1 all-reduce.2
  358.9 101.1 all-reduce.4
  462.9 31.0 reduce-scatter.1
where the time goes:
time: 504 us; the launch traced here: 501 us
  waiting for transfers between devices  202 us (40%)
  local copies, waits for them, and re-layouts  133 us (26%)
  other arithmetic  75.4 us (15%)
  matrix products  34.7 us (7%)
  loops' own time  31.3 us (6%)
  between operations  14.5 us (3%)
  starting transfers between devices  9.57 us (2%)
    psum x1, waiting for transfers between devices, body(): probe_grad = lax.psum(probe_terms, 'tile')  96.2 us
    psum x1, waiting for transfers between devices, body(): model_intensity = lax.psum(partial_intensity, 'mode')  74.5 us
    dynamic_update_slice x8, local copies, waits for them, and re-layouts, place_one(): lax.dynamic_update_slice(current, old_values + terms[:, position], anchor)  48.3 us
    dot_general x2, matrix products, transform(): jnp.einsum('bpmrc,abck->apmrk', half_pass, blocks_table, preferred_elemen...  34.7 us
    gather x24, local copies, waits for them, and re-layouts  32.3 us
    another operation x1, loops' own time, place_terms(): return lax.fori_loop(0, terms.shape[1], place_one, accumulated)  31.2 us
    reduce_scatter x1, waiting for transfers between devices, body(): lax.psum_scatter(interior, 'mode', scatter_dimension=2, tiled=True)  31.1 us
    add x1, other arithmetic, conj_times(): left_factor[0] * right_factor[0] + left_factor[1] * right_factor[1]  17.7 us
  transfers between devices with their start and end apart: 7, of which 3 were waited for; matrix products, arithmetic and copies ran while one was open for 6% of the time, Pallas kernels for 0%

commit v1 on v0

v1 whole, which is shorter than its diff:
```python
import functools
import math

import jax
import jax.numpy as jnp
import numpy as np
from jax import lax
from jax.experimental import pallas as pl
from jax.experimental.pallas import tpu as pltpu
from jax.sharding import PartitionSpec as P

MESH = pl.DeviceIdType.MESH
MIB = 1024 * 1024
F32 = jnp.float32
BF16 = jnp.bfloat16


def dft_tables(window):
    index = np.arange(window)
    angles = (index[:, None] * index[None, :] % window) * (2.0 * math.pi / window)
    cr = np.cos(angles) / math.sqrt(window)
    ci = -np.sin(angles) / math.sqrt(window)
    left = np.block([[cr, -ci], [ci, cr]])
    right = np.block([[cr, ci], [-ci, cr]])
    return jnp.asarray(left, BF16), jnp.asarray(right, BF16)


def gather_kernel(tiles, peers, half, obj, prb, above, below, allp, halo_s, halo_r, prb_s, prb_r, fwd_s, fwd_r, loc):
    t = lax.axis_index("tile")
    m = lax.axis_index("mode")
    sib = t + 1 - 2 * (t % 2)
    c = t % 2
    tile_rows = obj.shape[1]
    nm = prb.shape[1]
    win = prb.shape[2]
    hw = win // 2
    barrier = pltpu.get_barrier_semaphore()

    def hello(tt, mm):
        pl.semaphore_signal(barrier, inc=1, device_id=(tt, mm), device_id_type=MESH)

    @pl.when(t > 0)
    def _():
        hello(t - 1, m)

    @pl.when(t < tiles - 1)
    def _():
        hello(t + 1, m)

    for d in range(1, peers):
        hello(t, (m + d) % peers)
    pl.semaphore_wait(barrier, peers - 1 + (t + tiles - 1) // tiles + (2 * tiles - 2 - t) // tiles)

    own = pltpu.make_async_copy(prb, allp.at[:, pl.ds(m * nm, nm)], loc)

    def probe_copy(d, part):
        return pltpu.make_async_remote_copy(
            src_ref=prb.at[part, :, pl.ds(c * hw, hw)],
            dst_ref=allp.at[part, pl.ds(m * nm, nm), pl.ds(c * hw, hw)],
            send_sem=prb_s.at[d - 1, part],
            recv_sem=prb_r.at[d - 1, part],
            device_id=(t, (m + d) % peers),
            device_id_type=MESH,
        )

    def forward_copy(d, part, core):
        src = (m - d + peers) % peers
        view = allp.at[part, pl.ds(src * nm, nm), pl.ds(core * hw, hw)]
        return pltpu.make_async_remote_copy(
            src_ref=view,
            dst_ref=view,
            send_sem=fwd_s.at[d - 1, part],
            recv_sem=fwd_r.at[d - 1, part],
            device_id=(sib, m),
            device_id_type=MESH,
        )

    up = pltpu.make_async_remote_copy(
        src_ref=obj.at[:, pl.ds(tile_rows - half, half)], dst_ref=above,
        send_sem=halo_s.at[0], recv_sem=halo_r.at[0], device_id=(t + 1, m), device_id_type=MESH)
    down = pltpu.make_async_remote_copy(
        src_ref=obj.at[:, pl.ds(0, half)], dst_ref=below,
        send_sem=halo_s.at[1], recv_sem=halo_r.at[1], device_id=(t - 1, m), device_id_type=MESH)

    @pl.when(t < tiles - 1)
    def _():
        up.start()

    @pl.when(t > 0)
    def _():
        down.start()

    for d in range(1, peers):
        for part in range(2):
            probe_copy(d, part).start()
    own.start()
    for d in range(1, peers):
        for part in range(2):
            probe_copy(d, part).wait_recv()
            forward_copy(d, part, c).start()
    for d in range(1, peers):
        for part in range(2):
            forward_copy(d, part, 1 - c).wait_recv()
            forward_copy(d, part, c).wait_send()
            probe_copy(d, part).wait_send()
    own.wait()

    @pl.when(t > 0)
    def _():
        up.wait_recv()
        down.wait_send()

    @pl.when(t < tiles - 1)
    def _():
        down.wait_recv()
        up.wait_send()


def gather(obj, prb, tiles, peers, half):
    cols = obj.shape[2]
    nm, win = prb.shape[1:3]
    dma = pltpu.SemaphoreType.DMA
    anyspace = pl.BlockSpec(memory_space=pl.ANY)
    return pl.pallas_call(
        functools.partial(gather_kernel, tiles, peers, half),
        out_shape=(
            jax.ShapeDtypeStruct((2, half, cols), F32),
            jax.ShapeDtypeStruct((2, half, cols), F32),
            jax.ShapeDtypeStruct((2, nm * peers, win, win), F32),
        ),
        in_specs=[anyspace, anyspace],
        out_specs=(anyspace, anyspace, anyspace),
        scratch_shapes=[dma((2,)), dma((2,)), dma((peers - 1, 2)), dma((peers - 1, 2)),
                        dma((peers - 1, 2)), dma((peers - 1, 2)), dma],
        compiler_params=pltpu.CompilerParams(collective_id=1, has_side_effects=True),
    )(obj, prb)


def compute_kernel(half, rows, cols, live, me, above, obj, below, prb, measured, left, right,
                   grad, pgrad, padded, far, patch, terms, meas, sems):
    peers = me[1]
    m = me[0]
    win = patch.shape[1]
    tile_rows = obj.shape[1]
    modes = prb.shape[1]
    copies = [
        pltpu.make_async_copy(above, padded.at[:, pl.ds(0, half)], sems.at[0]),
        pltpu.make_async_copy(obj, padded.at[:, pl.ds(half, tile_rows)], sems.at[1]),
        pltpu.make_async_copy(below, padded.at[:, pl.ds(half + tile_rows, half)], sems.at[2]),
    ]
    for copy in copies:
        copy.start()
    grad[...] = jnp.zeros(grad.shape, F32)
    pgrad[...] = jnp.zeros(pgrad.shape, F32)
    for copy in copies:
        copy.wait()
    count = (live[0] - m + peers - 1) // peers

    def position(i, carry):
        slot = m + i * peers
        fetch = pltpu.make_async_copy(measured.at[slot], meas.at[0], sems.at[3])
        fetch.start()
        row = rows[slot] + half
        col = cols[slot]
        base = pl.multiple_of(jnp.minimum(col // 128, (padded.shape[2] - win - 128) // 128) * 128, 128)
        shift = col - base
        wide = win + 128
        tall = win + 8
        top = pl.multiple_of(jnp.minimum(row // 8, (padded.shape[1] - tall) // 8) * 8, 8)
        drop = row - top
        for part in range(2):
            block = padded[part, pl.ds(top, tall), pl.ds(base, wide)]
            block = pltpu.roll(block, (tall - drop) % tall, 0)[:win]
            patch[part] = pltpu.roll(block, (wide - shift) % wide, 1)[:, :win]
        meas[1] = jnp.zeros((win, win), F32)

        def forward(pair, carry):
            pr, pi = patch[0], patch[1]
            exits = []
            for k in range(2):
                qr, qi = prb[0, 2 * pair + k], prb[1, 2 * pair + k]
                er = (qr * pr - qi * pi).astype(BF16)
                ei = (qr * pi + qi * pr).astype(BF16)
                exits.append(jnp.concatenate([er, ei], axis=0))
            wave = jnp.concatenate(exits, axis=1)
            halfp = jnp.dot(left[...], wave, preferred_element_type=F32).astype(BF16)
            for k in range(2):
                lhs = jnp.concatenate(
                    [halfp[:win, k * win:(k + 1) * win], halfp[win:, k * win:(k + 1) * win]], axis=1)
                out = jnp.dot(lhs, right[...], preferred_element_type=F32)
                far[2 * pair + k] = out
                fr, fi = out[:, :win], out[:, win:]
                meas[1] += fr * fr + fi * fi
            return carry

        lax.fori_loop(0, modes // 2, forward, 0)
        fetch.wait()
        meas[1] = 1.0 - jnp.sqrt(meas[0]) / jnp.maximum(jnp.sqrt(meas[1]), 0.5)
        terms[...] = jnp.zeros(terms.shape, F32)

        def backward(pair, carry):
            scaling = meas[1]
            chis = []
            for k in range(2):
                value = far[2 * pair + k]
                chis.append(jnp.concatenate(
                    [(value[:, :win] * scaling).astype(BF16), (value[:, win:] * scaling).astype(BF16)], axis=0))
            wave = jnp.concatenate(chis, axis=1)
            halfp = jnp.dot(right[...], wave, preferred_element_type=F32).astype(BF16)
            for k in range(2):
                mode = 2 * pair + k
                lhs = jnp.concatenate(
                    [halfp[:win, k * win:(k + 1) * win], halfp[win:, k * win:(k + 1) * win]], axis=1)
                back = jnp.dot(lhs, left[...], preferred_element_type=F32)
                br, bi = back[:, :win], back[:, win:]
                pr, pi = patch[0], patch[1]
                qr, qi = prb[0, mode], prb[1, mode]
                terms[0, :win, :win] += qr * br + qi * bi
                terms[1, :win, :win] += qr * bi - qi * br
                pgrad[0, mode] += pr * br + pi * bi
                pgrad[1, mode] += pr * bi - pi * br
            return carry

        lax.fori_loop(0, modes // 2, backward, 0)
        for part in range(2):
            grad[part, pl.ds(top, tall), pl.ds(base, wide)] += pltpu.roll(pltpu.roll(terms[part], shift, 1), drop, 0)
        return carry

    lax.fori_loop(0, count, position, 0)


def compute(rows, cols, live, me, above, obj, below, prb, measured, half):
    win = prb.shape[2]
    modes = prb.shape[1]
    left, right = dft_tables(win)
    anyspace = pl.BlockSpec(memory_space=pl.ANY)
    smem = pl.BlockSpec(memory_space=pltpu.SMEM)
    vmem = pl.BlockSpec(memory_space=pltpu.VMEM)
    height = obj.shape[1] + 2 * half
    return pl.pallas_call(
        functools.partial(compute_kernel, half),
        out_shape=(
            jax.ShapeDtypeStruct((2, height, obj.shape[2]), F32),
            jax.ShapeDtypeStruct(prb.shape, F32),
        ),
        in_specs=[smem, smem, smem, smem, anyspace, anyspace, anyspace, vmem, anyspace, vmem, vmem],
        out_specs=(vmem, vmem),
        scratch_shapes=[
            pltpu.VMEM((2, height, obj.shape[2]), F32),
            pltpu.VMEM((modes, win, 2 * win), F32),
            pltpu.VMEM((2, win, win), F32),
            pltpu.VMEM((2, win + 8, win + 128), F32),
            pltpu.VMEM((2, win, win), F32),
            pltpu.SemaphoreType.DMA((4,)),
        ],
        compiler_params=pltpu.CompilerParams(vmem_limit_bytes=48 * MIB),
    )(rows, cols, live, me, above, obj, below, prb, measured, left, right)


def reduce_kernel(tiles, peers, half, grad, pgrad, ograd, oprobe,
                  edge, sibp, modep, mine, chipp, objp,
                  edge_s, edge_r, sib_s, sib_r, mode_s, mode_r, chip_s, chip_r, obj_s, obj_r, ag_s, ag_r, fw_s, fw_r):
    t = lax.axis_index("tile")
    m = lax.axis_index("mode")
    c = t % 2
    q = t // 2
    chips = tiles // 2
    sib = t + 1 - 2 * c
    modes, win = pgrad.shape[1:3]
    nm = modes // peers
    hw = win // 2
    tile_rows = ograd.shape[1]
    width = ograd.shape[2]
    rows = hw // chips
    barrier = pltpu.get_barrier_semaphore()

    def hello(tt, mm):
        pl.semaphore_signal(barrier, inc=1, device_id=(tt, mm), device_id_type=MESH)

    def chip_tile(d):
        return ((q + d) % chips) * 2 + c

    @pl.when(t > 0)
    def _():
        hello(t - 1, m)

    @pl.when(t < tiles - 1)
    def _():
        hello(t + 1, m)

    for d in range(1, peers):
        hello(t, (m + d) % peers)
    for d in range(1, chips):
        hello(chip_tile(d), m)
    pl.semaphore_wait(barrier, peers + chips - 2 + (t + tiles - 1) // tiles + (2 * tiles - 2 - t) // tiles)

    def remote(src, dst, ssem, rsem, tt, mm):
        return pltpu.make_async_remote_copy(
            src_ref=src, dst_ref=dst, send_sem=ssem, recv_sem=rsem,
            device_id=(tt, mm), device_id_type=MESH)

    to_next = remote(grad.at[:, pl.ds(half + tile_rows, half)], edge.at[0], edge_s.at[0], edge_r.at[0], t + 1, m)
    to_prev = remote(grad.at[:, pl.ds(0, half)], edge.at[1], edge_s.at[1], edge_r.at[1], t - 1, m)

    def sib_copy(d):
        group = ((m + d) % peers) * nm
        return remote(pgrad.at[:, pl.ds(group, nm), pl.ds((1 - c) * hw, hw)], sibp.at[d],
                      sib_s.at[d], sib_r.at[d], sib, m)

    def mode_copy(d):
        return remote(sibp.at[d], modep.at[d - 1], mode_s.at[d - 1], mode_r.at[d - 1], t, (m + d) % peers)

    def chip_copy(d):
        k = (q + d) % chips
        return remote(mine.at[:, :, pl.ds(k * rows, rows)], chipp.at[d - 1],
                      chip_s.at[d - 1], chip_r.at[d - 1], chip_tile(d), m)

    def obj_copy(d, upper):
        column = ((m + d) % peers) * width
        hr = tile_rows // 2
        return remote(grad.at[:, pl.ds(half + upper * hr, hr), pl.ds(column, width)],
                      objp.at[d - 1, :, pl.ds(upper * hr, hr)],
                      obj_s.at[d - 1, upper], obj_r.at[d - 1, upper], t, (m + d) % peers)

    def out_view(core, chip):
        return oprobe.at[:, :, pl.ds(core * hw + chip * rows, rows)]

    def ag_copy(d):
        return remote(out_view(c, q), out_view(c, q), ag_s.at[d - 1], ag_r.at[d - 1], chip_tile(d), m)

    def fw_copy(d, core):
        chip = (q - d + chips) % chips
        return remote(out_view(core, chip), out_view(core, chip), fw_s.at[d], fw_r.at[d], sib, m)

    for d in list(range(1, peers)) + [0]:
        sib_copy(d).start()

    @pl.when(t < tiles - 1)
    def _():
        to_next.start()

    @pl.when(t > 0)
    def _():
        to_prev.start()

    for d in range(1, peers):
        group = ((m + d) % peers) * nm
        sib_copy(d).wait_recv()
        sibp[d] += pgrad[:, pl.ds(group, nm), pl.ds(c * hw, hw)]
        mode_copy(d).start()
    sib_copy(0).wait_recv()
    mine[...] = sibp[0] + pgrad[:, pl.ds(m * nm, nm), pl.ds(c * hw, hw)]

    @pl.when(t > 0)
    def _():
        to_next.wait_recv()
        grad[:, pl.ds(half, half)] += edge[0]

    for d in range(1, peers):
        obj_copy(d, 0).start()

    @pl.when(t < tiles - 1)
    def _():
        to_prev.wait_recv()
        grad[:, pl.ds(tile_rows, half)] += edge[1]

    for d in range(1, peers):
        obj_copy(d, 1).start()
    for d in range(1, peers):
        mode_copy(d).wait_recv()
        mine[...] += modep[d - 1]
    for d in range(1, chips):
        chip_copy(d).start()
    total = mine[:, :, pl.ds(q * rows, rows)]
    for d in range(1, chips):
        chip_copy(d).wait_recv()
        total += chipp[d - 1]
    oprobe[:, :, pl.ds(c * hw + q * rows, rows)] = total
    for d in range(1, chips):
        ag_copy(d).start()
    fw_copy(0, c).start()
    for d in range(1, chips):
        ag_copy(d).wait_recv()
        fw_copy(d, c).start()

    ograd[...] = grad[:, pl.ds(half, tile_rows), pl.ds(pl.multiple_of(m * width, 128), width)]
    for d in range(1, peers):
        for upper in range(2):
            obj_copy(d, upper).wait_recv()
        ograd[...] += objp[d - 1]
    for d in range(chips):
        fw_copy(d, 1 - c).wait_recv()
        fw_copy(d, c).wait_send()

    @pl.when(t < tiles - 1)
    def _():
        to_next.wait_send()

    @pl.when(t > 0)
    def _():
        to_prev.wait_send()

    for d in range(peers):
        sib_copy(d).wait_send()
    for d in range(1, peers):
        mode_copy(d).wait_send()
        for upper in range(2):
            obj_copy(d, upper).wait_send()
    for d in range(1, chips):
        chip_copy(d).wait_send()
        ag_copy(d).wait_send()


def reduce(grad, pgrad, tiles, peers, half):
    modes, win = pgrad.shape[1:3]
    nm, hw = modes // peers, win // 2
    chips = tiles // 2
    rows = hw // chips
    tile_rows = grad.shape[1] - 2 * half
    cols = grad.shape[2]
    width = cols // peers
    dma = pltpu.SemaphoreType.DMA
    vmem = pl.BlockSpec(memory_space=pltpu.VMEM)
    return pl.pallas_call(
        functools.partial(reduce_kernel, tiles, peers, half),
        out_shape=(
            jax.ShapeDtypeStruct((2, tile_rows, width), F32),
            jax.ShapeDtypeStruct((2, nm, win, win), F32),
        ),
        in_specs=[vmem, vmem],
        out_specs=(vmem, vmem),
        scratch_shapes=[
            pltpu.VMEM((2, 2, half, cols), F32),
            pltpu.VMEM((peers, 2, nm, hw, win), F32),
            pltpu.VMEM((peers - 1, 2, nm, hw, win), F32),
            pltpu.VMEM((2, nm, hw, win), F32),
            pltpu.VMEM((chips - 1, 2, nm, rows, win), F32),
            pltpu.VMEM((peers - 1, 2, tile_rows, width), F32),
            dma((2,)), dma((2,)), dma((peers,)), dma((peers,)), dma((peers - 1,)), dma((peers - 1,)),
            dma((chips - 1,)), dma((chips - 1,)), dma((peers - 1, 2)), dma((peers - 1, 2)),
            dma((chips - 1,)), dma((chips - 1,)), dma((chips,)), dma((chips,)),
        ],
        compiler_params=pltpu.CompilerParams(
            collective_id=2, has_side_effects=True, vmem_limit_bytes=48 * MIB),
    )(grad, pgrad)


def body(object_field, probe_modes, measured, row_starts, col_starts, live_counts):
    tiles, peers = lax.axis_size("tile"), lax.axis_size("mode")
    half = probe_modes.shape[-1] // 2
    above, below, allp = gather(object_field, probe_modes, tiles, peers, half)
    me = jnp.stack([lax.axis_index("mode").astype(jnp.int32), jnp.int32(peers)])
    grad, pgrad = compute(row_starts, col_starts, live_counts, me, above, object_field, below, allp, measured, half)
    return reduce(grad, pgrad, tiles, peers, half)


def solution(mesh):
    return jax.shard_map(
        body,
        mesh=mesh,
        in_specs=(
            P(None, "tile", None),
            P(None, "mode", None, None),
            P("tile", None, None),
            P("tile"),
            P("tile"),
            P("tile"),
        ),
        out_specs=(P(None, "tile", "mode"), P(None, "mode", None, None)),
        check_vma=False,
    )
```

time: 504 us -> 196 us (0.39)
  the two profiles are of different devices: /device:TPU:0 before, /device:TPU:27 now
where the time goes in v1:
time: 196 us; the launch traced here: 195 us
  Pallas kernels  189 us (96%)
  local copies, waits for them, and re-layouts  4.75 us (2%)
    pallas_call x1, Pallas kernels, reduce(): pl.pallas_call(functools.partial(reduce_kernel, tiles, peers, half), out_...  84.2 us
    pallas_call x1, Pallas kernels, gather(): pl.pallas_call(functools.partial(gather_kernel, tiles, peers, half), out_...  66 us
    pallas_call x1, Pallas kernels, compute(): pl.pallas_call(functools.partial(compute_kernel, half), out_shape=(jax.Sh...  38.5 us
    unnamed x16, local copies, waits for them, and re-layouts  4.75 us

profile of v1, /device:TPU:27, one launch (start us, length us, event | category | flops | bytes accessed | tf_op | source)
XLA Modules:
  0.0 194.9 jit_solution(3054544804649813226)
XLA Ops:
  1.3 0.1 pad_add_fusion.me
  1.4 0.0 copy-start
  1.4 0.0 copy-start.3
  1.4 0.0 copy-start.4
  1.4 0.0 copy-start.5
  1.4 0.0 copy-start.6
  1.4 66.0 %shard_map.95 = (f32[2,128,1024]{2,1,0:T(8,128)}, f32[2,128,1024]{2,1,0:T(8,128)}, f32[2,8,256,256]{3,2,1,0:T(8,128)}) custom-call(f32[2,256,1024]{2,1,0:T(8,128)} %obj.3, f32[2,4,256,256]{3,2,1,0:T(8,128)} %prb.1), custom_call_target="tpu_custom_call" | custom-call | tf_op jit(solution)/shard_map/pallas_call | solution.py:124
  67.4 0.0 copy-done
  67.4 0.0 copy-done.3
  67.4 0.0 copy-done.4
  67.5 0.0 copy-done.5
  67.5 0.0 copy-done.6
  67.5 0.0 copy-start.1
  67.5 1.2 copy-done.1
  68.7 0.0 copy-start.2
  68.7 1.2 copy-done.2
  69.9 38.5 %shard_map.96 = (f32[2,512,1024]{2,1,0:T(8,128)}, f32[2,8,256,256]{3,2,1,0:T(8,128)}) custom-call(s32[8]{0:T(128)S(1)} %copy-done.5, s32[8]{0:T(128)S(1)} %copy-done.6, s32[1]{0:T(128)S(6)} %copy.12.live, s32[2]{0:T(128)S(1)} %pad_add_fusion.me, f32[2,128,1024]{2,1,0:T(8,128)S(1)} %copy-done.1, f32[2,256,1024]{2,1,0:T(8,128)S(1)} %copy-done, ...), custom_call_target="tpu_custom_call" | custom-call | tf_op jit(solution)/shard_map/pallas_call | solution.py:240
  108.4 84.2 %shard_map.97 = (f32[2,256,512]{2,1,0:T(8,128)S(1)}, f32[2,4,256,256]{3,2,1,0:T(8,128)S(1)}) custom-call(f32[2,512,1024]{2,1,0:T(8,128)} %get-tuple-element.10.grad, f32[2,8,256,256]{3,2,1,0:T(8,128)} %get-tuple-element.11.pgrad), custom_call_target="tpu_custom_call" | custom-call | tf_op jit(solution)/shard_map/pallas_call | solution.py:424
  192.6 1.0 copy.13
  193.6 1.3 copy.14
Async XLA Ops:
  1.4 66.1 %copy-start = (f32[2,256,1024]{2,1,0:T(8,128)S(1)}, f32[2,256,1024]{2,1,0:T(8,128)}, u32[]{:S(2)}) copy-start(f32[2,256,1024]{2,1,0:T(8,128)} %obj.3) | copy-start | bytes 6291460
  1.4 66.1 %copy-start.3 = (bf16[512,512]{1,0:T(8,128)(2,1)S(1)}, bf16[512,512]{1,0:T(8,128)(2,1)}, u32[]{:S(2)}) copy-start(bf16[512,512]{1,0:T(8,128)(2,1)} %constant.11.clone.right) | copy-start | bytes 1572868
  1.4 66.1 %copy-start.4 = (bf16[512,512]{1,0:T(8,128)(2,1)S(1)}, bf16[512,512]{1,0:T(8,128)(2,1)}, u32[]{:S(2)}) copy-start(bf16[512,512]{1,0:T(8,128)(2,1)} %constant.10.clone.left) | copy-start | bytes 1572868
  1.4 66.1 %copy-start.5 = (s32[8]{0:T(128)S(1)}, s32[8]{0:T(128)}, u32[]{:S(2)}) copy-start(s32[8]{0:T(128)} %rows.1) | copy-start | bytes 100
  1.4 66.1 %copy-start.6 = (s32[8]{0:T(128)S(1)}, s32[8]{0:T(128)}, u32[]{:S(2)}) copy-start(s32[8]{0:T(128)} %cols.1) | copy-start | bytes 100
  67.5 1.2 copy-start.1
  68.7 1.2 copy-start.2

commit v2 on v1

--- a/solution.py
+++ b/solution.py
@@ -25,7 +25,7 @@
     return jnp.asarray(left, BF16), jnp.asarray(right, BF16)
 
 
-def gather_kernel(tiles, peers, half, obj, prb, above, below, allp, halo_s, halo_r, prb_s, prb_r, fwd_s, fwd_r, loc):
+def gather_kernel(tiles, peers, half, obj, prb, above, below, allp, halo_s, halo_r, prb_s, prb_r, fwd_s, fwd_r):
     t = lax.axis_index("tile")
     m = lax.axis_index("mode")
     sib = t + 1 - 2 * (t % 2)
@@ -50,8 +50,6 @@
     for d in range(1, peers):
         hello(t, (m + d) % peers)
     pl.semaphore_wait(barrier, peers - 1 + (t + tiles - 1) // tiles + (2 * tiles - 2 - t) // tiles)
-
-    own = pltpu.make_async_copy(prb, allp.at[:, pl.ds(m * nm, nm)], loc)
 
     def probe_copy(d, part):
         return pltpu.make_async_remote_copy(
@@ -93,7 +91,6 @@
     for d in range(1, peers):
         for part in range(2):
             probe_copy(d, part).start()
-    own.start()
     for d in range(1, peers):
         for part in range(2):
             probe_copy(d, part).wait_recv()
@@ -103,7 +100,6 @@
             forward_copy(d, part, 1 - c).wait_recv()
             forward_copy(d, part, c).wait_send()
             probe_copy(d, part).wait_send()
-    own.wait()
 
     @pl.when(t > 0)
     def _():
@@ -131,15 +127,15 @@
         in_specs=[anyspace, anyspace],
         out_specs=(anyspace, anyspace, anyspace),
         scratch_shapes=[dma((2,)), dma((2,)), dma((peers - 1, 2)), dma((peers - 1, 2)),
-                        dma((peers - 1, 2)), dma((peers - 1, 2)), dma],
+                        dma((peers - 1, 2)), dma((peers - 1, 2))],
         compiler_params=pltpu.CompilerParams(collective_id=1, has_side_effects=True),
     )(obj, prb)
 
 
-def compute_kernel(half, rows, cols, live, me, above, obj, below, prb, measured, left, right,
-                   grad, pgrad, padded, far, patch, terms, meas, sems):
-    peers = me[1]
+def compute_kernel(half, peers, rows, cols, live, me, above, obj, below, allp, own, measured, left, right,
+                   grad, pgrad, padded, prb, far, patch, terms, meas, sems, psems):
     m = me[0]
+    nm = own.shape[1]
     win = patch.shape[1]
     tile_rows = obj.shape[1]
     modes = prb.shape[1]
@@ -148,6 +144,10 @@
         pltpu.make_async_copy(obj, padded.at[:, pl.ds(half, tile_rows)], sems.at[1]),
         pltpu.make_async_copy(below, padded.at[:, pl.ds(half + tile_rows, half)], sems.at[2]),
     ]
+    copies.append(pltpu.make_async_copy(own, prb.at[:, pl.ds(m * nm, nm)], psems.at[0]))
+    for d in range(1, peers):
+        group = pl.ds((m + d) % peers * nm, nm)
+        copies.append(pltpu.make_async_copy(allp.at[:, group], prb.at[:, group], psems.at[d]))
     for copy in copies:
         copy.start()
     grad[...] = jnp.zeros(grad.shape, F32)
@@ -229,56 +229,61 @@
     lax.fori_loop(0, count, position, 0)
 
 
-def compute(rows, cols, live, me, above, obj, below, prb, measured, half):
-    win = prb.shape[2]
-    modes = prb.shape[1]
+def compute(rows, cols, live, me, above, obj, below, allp, own, measured, half):
+    modes, win = allp.shape[1:3]
+    peers = modes // own.shape[1]
     left, right = dft_tables(win)
     anyspace = pl.BlockSpec(memory_space=pl.ANY)
     smem = pl.BlockSpec(memory_space=pltpu.SMEM)
     vmem = pl.BlockSpec(memory_space=pltpu.VMEM)
     height = obj.shape[1] + 2 * half
     return pl.pallas_call(
-        functools.partial(compute_kernel, half),
+        functools.partial(compute_kernel, half, peers),
         out_shape=(
             jax.ShapeDtypeStruct((2, height, obj.shape[2]), F32),
-            jax.ShapeDtypeStruct(prb.shape, F32),
+            jax.ShapeDtypeStruct(allp.shape, F32),
         ),
-        in_specs=[smem, smem, smem, smem, anyspace, anyspace, anyspace, vmem, anyspace, vmem, vmem],
+        in_specs=[smem, smem, smem, smem, anyspace, anyspace, anyspace, anyspace, anyspace, anyspace, vmem, vmem],
         out_specs=(vmem, vmem),
         scratch_shapes=[
             pltpu.VMEM((2, height, obj.shape[2]), F32),
+            pltpu.VMEM(allp.shape, F32),
             pltpu.VMEM((modes, win, 2 * win), F32),
             pltpu.VMEM((2, win, win), F32),
             pltpu.VMEM((2, win + 8, win + 128), F32),
             pltpu.VMEM((2, win, win), F32),
             pltpu.SemaphoreType.DMA((4,)),
+            pltpu.SemaphoreType.DMA((peers,)),
         ],
         compiler_params=pltpu.CompilerParams(vmem_limit_bytes=48 * MIB),
-    )(rows, cols, live, me, above, obj, below, prb, measured, left, right)
+    )(rows, cols, live, me, above, obj, below, allp, own, measured, left, right)
 
 
 def reduce_kernel(tiles, peers, half, grad, pgrad, ograd, oprobe,
-                  edge, sibp, modep, mine, chipp, objp,
-                  edge_s, edge_r, sib_s, sib_r, mode_s, mode_r, chip_s, chip_r, obj_s, obj_r, ag_s, ag_r, fw_s, fw_r):
+                  edge, sibp, modep, mine, nearp, farp, objp,
+                  edge_s, edge_r, sib_s, sib_r, mode_s, mode_r, near_s, near_r, far_s, far_r,
+                  obj_s, obj_r, back_near_s, back_near_r, back_far_s, back_far_r, fw_s, fw_r):
     t = lax.axis_index("tile")
     m = lax.axis_index("mode")
     c = t % 2
-    q = t // 2
-    chips = tiles // 2
+    lo = t // 2 % 2
+    hi = t // 4
+    highs = tiles // 4
     sib = t + 1 - 2 * c
+    near = t + 2 - 4 * lo
     modes, win = pgrad.shape[1:3]
     nm = modes // peers
     hw = win // 2
     tile_rows = ograd.shape[1]
     width = ograd.shape[2]
-    rows = hw // chips
+    fine = hw // 2 // highs
     barrier = pltpu.get_barrier_semaphore()
 
     def hello(tt, mm):
         pl.semaphore_signal(barrier, inc=1, device_id=(tt, mm), device_id_type=MESH)
 
-    def chip_tile(d):
-        return ((q + d) % chips) * 2 + c
+    def far_tile(d):
+        return (hi + d) % highs * 4 + lo * 2 + c
 
     @pl.when(t > 0)
     def _():
@@ -290,9 +295,10 @@
 
     for d in range(1, peers):
         hello(t, (m + d) % peers)
-    for d in range(1, chips):
-        hello(chip_tile(d), m)
-    pl.semaphore_wait(barrier, peers + chips - 2 + (t + tiles - 1) // tiles + (2 * tiles - 2 - t) // tiles)
+    for d in range(1, highs):
+        hello(far_tile(d), m)
+    hello(near, m)
+    pl.semaphore_wait(barrier, peers + highs - 1 + (t + tiles - 1) // tiles + (2 * tiles - 2 - t) // tiles)
 
     def remote(src, dst, ssem, rsem, tt, mm):
         return pltpu.make_async_remote_copy(
@@ -302,18 +308,14 @@
     to_next = remote(grad.at[:, pl.ds(half + tile_rows, half)], edge.at[0], edge_s.at[0], edge_r.at[0], t + 1, m)
     to_prev = remote(grad.at[:, pl.ds(0, half)], edge.at[1], edge_s.at[1], edge_r.at[1], t - 1, m)
 
-    def sib_copy(d):
+    def sib_copy(d, part):
         group = ((m + d) % peers) * nm
-        return remote(pgrad.at[:, pl.ds(group, nm), pl.ds((1 - c) * hw, hw)], sibp.at[d],
-                      sib_s.at[d], sib_r.at[d], sib, m)
-
-    def mode_copy(d):
-        return remote(sibp.at[d], modep.at[d - 1], mode_s.at[d - 1], mode_r.at[d - 1], t, (m + d) % peers)
-
-    def chip_copy(d):
-        k = (q + d) % chips
-        return remote(mine.at[:, :, pl.ds(k * rows, rows)], chipp.at[d - 1],
-                      chip_s.at[d - 1], chip_r.at[d - 1], chip_tile(d), m)
+        return remote(pgrad.at[part, pl.ds(group, nm), pl.ds((1 - c) * hw, hw)], sibp.at[d, part],
+                      sib_s.at[d, part], sib_r.at[d, part], sib, m)
+
+    def mode_copy(d, part):
+        return remote(sibp.at[d, part], modep.at[d - 1, part],
+                      mode_s.at[d - 1, part], mode_r.at[d - 1, part], t, (m + d) % peers)
 
     def obj_copy(d, upper):
         column = ((m + d) % peers) * width
@@ -322,18 +324,61 @@
                       objp.at[d - 1, :, pl.ds(upper * hr, hr)],
                       obj_s.at[d - 1, upper], obj_r.at[d - 1, upper], t, (m + d) % peers)
 
-    def out_view(core, chip):
-        return oprobe.at[:, :, pl.ds(core * hw + chip * rows, rows)]
-
-    def ag_copy(d):
-        return remote(out_view(c, q), out_view(c, q), ag_s.at[d - 1], ag_r.at[d - 1], chip_tile(d), m)
-
-    def fw_copy(d, core):
-        chip = (q - d + chips) % chips
-        return remote(out_view(core, chip), out_view(core, chip), fw_s.at[d], fw_r.at[d], sib, m)
-
-    for d in list(range(1, peers)) + [0]:
-        sib_copy(d).start()
+    def near_start(part, low, high):
+        return low * (hw // 2) if part == 0 else high * 2 * fine + low * fine
+
+    def far_start(part, low, high):
+        return low * (hw // 2) + high * fine if part == 0 else high * 2 * fine
+
+    near_rows = (hw // 2, fine)
+    far_rows = (fine, 2 * fine)
+
+    def near_copy(part):
+        rows = near_rows[part]
+        return remote(mine.at[part, :, pl.ds(near_start(part, 1 - lo, hi), rows)], nearp.at[part, :, pl.ds(0, rows)],
+                      near_s.at[part], near_r.at[part], near, m)
+
+    def far_copy(part, d):
+        rows = far_rows[part]
+        return remote(mine.at[part, :, pl.ds(far_start(part, lo, (hi + d) % highs), rows)],
+                      farp.at[part, d - 1, :, pl.ds(0, rows)],
+                      far_s.at[part, d - 1], far_r.at[part, d - 1], far_tile(d), m)
+
+    def add_near(part):
+        rows = near_rows[part]
+        near_copy(part).wait_recv()
+        mine[part, :, pl.ds(near_start(part, lo, hi), rows)] += nearp[part, :, pl.ds(0, rows)]
+
+    def add_far(part):
+        rows = far_rows[part]
+        keep = pl.ds(far_start(part, lo, hi), rows)
+        total = mine[part, :, keep]
+        for d in range(1, highs):
+            far_copy(part, d).wait_recv()
+            total += farp[part, d - 1, :, pl.ds(0, rows)]
+        mine[part, :, keep] = total
+
+    def settle(part):
+        start = lo * (hw // 2) + hi * fine if part == 0 else hi * 2 * fine + lo * fine
+        oprobe[part, :, pl.ds(c * hw + start, fine)] = mine[part, :, pl.ds(start, fine)]
+
+    def back_near(part):
+        view = oprobe.at[part, :, pl.ds(c * hw + near_start(part, lo, hi), near_rows[part])]
+        return remote(view, view, back_near_s.at[part], back_near_r.at[part], near, m)
+
+    def back_far(part, d):
+        view = oprobe.at[part, :, pl.ds(c * hw + far_start(part, lo, hi), far_rows[part])]
+        return remote(view, view, back_far_s.at[part, d - 1], back_far_r.at[part, d - 1], far_tile(d), m)
+
+    def fw_copy(part):
+        view = oprobe.at[part, :, pl.ds(c * hw, hw)]
+        return remote(view, view, fw_s.at[part], fw_r.at[part], sib, m)
+
+    for part in range(2):
+        for d in range(1, peers):
+            sib_copy(d, part).start()
+    for part in range(2):
+        sib_copy(0, part).start()
 
     @pl.when(t < tiles - 1)
     def _():
@@ -343,13 +388,20 @@
     def _():
         to_prev.start()
 
-    for d in range(1, peers):
-        group = ((m + d) % peers) * nm
-        sib_copy(d).wait_recv()
-        sibp[d] += pgrad[:, pl.ds(group, nm), pl.ds(c * hw, hw)]
-        mode_copy(d).start()
-    sib_copy(0).wait_recv()
-    mine[...] = sibp[0] + pgrad[:, pl.ds(m * nm, nm), pl.ds(c * hw, hw)]
+    for part in range(2):
+        for d in range(1, peers):
+            group = ((m + d) % peers) * nm
+            sib_copy(d, part).wait_recv()
+            sibp[d, part] += pgrad[part, pl.ds(group, nm), pl.ds(c * hw, hw)]
+            mode_copy(d, part).start()
+    for part in range(2):
+        sib_copy(0, part).wait_recv()
+        mine[part] = sibp[0, part] + pgrad[part, pl.ds(m * nm, nm), pl.ds(c * hw, hw)]
+
+    for d in range(1, peers):
+        mode_copy(d, 0).wait_recv()
+        mine[0] += modep[d - 1, 0]
+    near_copy(0).start()
 
     @pl.when(t > 0)
     def _():
@@ -367,30 +419,41 @@
     for d in range(1, peers):
         obj_copy(d, 1).start()
     for d in range(1, peers):
-        mode_copy(d).wait_recv()
-        mine[...] += modep[d - 1]
-    for d in range(1, chips):
-        chip_copy(d).start()
-    total = mine[:, :, pl.ds(q * rows, rows)]
-    for d in range(1, chips):
-        chip_copy(d).wait_recv()
-        total += chipp[d - 1]
-    oprobe[:, :, pl.ds(c * hw + q * rows, rows)] = total
-    for d in range(1, chips):
-        ag_copy(d).start()
-    fw_copy(0, c).start()
-    for d in range(1, chips):
-        ag_copy(d).wait_recv()
-        fw_copy(d, c).start()
+        mode_copy(d, 1).wait_recv()
+        mine[1] += modep[d - 1, 1]
+    for d in range(1, highs):
+        far_copy(1, d).start()
+    add_near(0)
+    for d in range(1, highs):
+        far_copy(0, d).start()
+    add_far(1)
+    near_copy(1).start()
+    add_far(0)
+    settle(0)
+    for d in range(1, highs):
+        back_far(0, d).start()
+    add_near(1)
+    settle(1)
+    back_near(1).start()
+    for d in range(1, highs):
+        back_far(0, d).wait_recv()
+    back_near(0).start()
+    back_near(1).wait_recv()
+    for d in range(1, highs):
+        back_far(1, d).start()
 
     ograd[...] = grad[:, pl.ds(half, tile_rows), pl.ds(pl.multiple_of(m * width, 128), width)]
+    back_near(0).wait_recv()
+    fw_copy(0).start()
+    for d in range(1, highs):
+        back_far(1, d).wait_recv()
+    fw_copy(1).start()
     for d in range(1, peers):
         for upper in range(2):
             obj_copy(d, upper).wait_recv()
         ograd[...] += objp[d - 1]
-    for d in range(chips):
-        fw_copy(d, 1 - c).wait_recv()
-        fw_copy(d, c).wait_send()
+    for part in range(2):
+        fw_copy(part).wait_recv()
 
     @pl.when(t < tiles - 1)
     def _():
@@ -400,22 +463,24 @@
     def _():
         to_prev.wait_send()
 
-    for d in range(peers):
-        sib_copy(d).wait_send()
-    for d in range(1, peers):
-        mode_copy(d).wait_send()
-        for upper in range(2):
-            obj_copy(d, upper).wait_send()
-    for d in range(1, chips):
-        chip_copy(d).wait_send()
-        ag_copy(d).wait_send()
+    for part in range(2):
+        fw_copy(part).wait_send()
+        near_copy(part).wait_send()
+        back_near(part).wait_send()
+        for d in range(peers):
+            sib_copy(d, part).wait_send()
+        for d in range(1, peers):
+            mode_copy(d, part).wait_send()
+            obj_copy(d, part).wait_send()
+        for d in range(1, highs):
+            far_copy(part, d).wait_send()
+            back_far(part, d).wait_send()
 
 
 def reduce(grad, pgrad, tiles, peers, half):
     modes, win = pgrad.shape[1:3]
     nm, hw = modes // peers, win // 2
-    chips = tiles // 2
-    rows = hw // chips
+    highs = tiles // 4
     tile_rows = grad.shape[1] - 2 * half
     cols = grad.shape[2]
     width = cols // peers
@@ -434,11 +499,13 @@
             pltpu.VMEM((peers, 2, nm, hw, win), F32),
             pltpu.VMEM((peers - 1, 2, nm, hw, win), F32),
             pltpu.VMEM((2, nm, hw, win), F32),
-            pltpu.VMEM((chips - 1, 2, nm, rows, win), F32),
+            pltpu.VMEM((2, nm, hw // 2, win), F32),
+            pltpu.VMEM((2, highs - 1, nm, hw // highs, win), F32),
             pltpu.VMEM((peers - 1, 2, tile_rows, width), F32),
-            dma((2,)), dma((2,)), dma((peers,)), dma((peers,)), dma((peers - 1,)), dma((peers - 1,)),
-            dma((chips - 1,)), dma((chips - 1,)), dma((peers - 1, 2)), dma((peers - 1, 2)),
-            dma((chips - 1,)), dma((chips - 1,)), dma((chips,)), dma((chips,)),
+            dma((2,)), dma((2,)), dma((peers, 2)), dma((peers, 2)), dma((peers - 1, 2)), dma((peers - 1, 2)),
+            dma((2,)), dma((2,)), dma((2, highs - 1)), dma((2, highs - 1)),
+            dma((peers - 1, 2)), dma((peers - 1, 2)),
+            dma((2,)), dma((2,)), dma((2, highs - 1)), dma((2, highs - 1)), dma((2,)), dma((2,)),
         ],
         compiler_params=pltpu.CompilerParams(
             collective_id=2, has_side_effects=True, vmem_limit_bytes=48 * MIB),
@@ -449,8 +516,8 @@
     tiles, peers = lax.axis_size("tile"), lax.axis_size("mode")
     half = probe_modes.shape[-1] // 2
     above, below, allp = gather(object_field, probe_modes, tiles, peers, half)
-    me = jnp.stack([lax.axis_index("mode").astype(jnp.int32), jnp.int32(peers)])
-    grad, pgrad = compute(row_starts, col_starts, live_counts, me, above, object_field, below, allp, measured, half)
+    me = lax.axis_index("mode").astype(jnp.int32).reshape(1)
+    grad, pgrad = compute(row_starts, col_starts, live_counts, me, above, object_field, below, allp, probe_modes, measured, half)
     return reduce(grad, pgrad, tiles, peers, half)
 
 

time: 196 us -> 145 us (0.74)
  the two profiles are of different devices: /device:TPU:27 before, /device:TPU:0 now
where the time goes in v2:
time: 145 us
  Pallas kernels  139 us (96%)
  local copies, waits for them, and re-layouts  4.76 us (3%)
    pallas_call x1, Pallas kernels, reduce(): pl.pallas_call(functools.partial(reduce_kernel, tiles, peers, half), out_...  95.3 us
    pallas_call x1, Pallas kernels, gather(): pl.pallas_call(functools.partial(gather_kernel, tiles, peers, half), out_...  29.1 us
    pallas_call x1, Pallas kernels, compute(): pl.pallas_call(functools.partial(compute_kernel, half, peers), out_shape=...  14.2 us
    unnamed x16, local copies, waits for them, and re-layouts  4.76 us

profile of v2, /device:TPU:0, one launch (start us, length us, event | category | flops | bytes accessed | tf_op | source)
XLA Modules:
  0.0 144.8 jit_solution(4632318166699927973)
XLA Ops:
  1.3 0.0 copy-start
  1.3 0.0 copy-start.3
  1.3 0.0 copy-start.4
  1.3 0.0 copy-start.5
  1.3 0.0 copy-start.6
  1.3 29.1 %shard_map.95 = (f32[2,128,1024]{2,1,0:T(8,128)}, f32[2,128,1024]{2,1,0:T(8,128)}, f32[2,8,256,256]{3,2,1,0:T(8,128)}) custom-call(f32[2,256,1024]{2,1,0:T(8,128)} %obj.3, f32[2,4,256,256]{3,2,1,0:T(8,128)} %own.1), custom_call_target="tpu_custom_call" | custom-call | tf_op jit(solution)/shard_map/pallas_call | solution.py:120
  30.4 0.0 copy-done
  30.4 0.0 copy-done.3
  30.4 0.0 copy-done.4
  30.4 0.0 copy-done.5
  30.4 0.0 copy-done.6
  30.5 0.0 copy-start.1
  30.5 1.2 copy-done.1
  31.7 0.0 copy-start.2
  31.7 1.2 copy-done.2
  32.9 14.2 %shard_map.96 = (f32[2,512,1024]{2,1,0:T(8,128)}, f32[2,8,256,256]{3,2,1,0:T(8,128)}) custom-call(s32[8]{0:T(128)S(1)} %copy-done.5, s32[8]{0:T(128)S(1)} %copy-done.6, s32[1]{0:T(128)S(6)} %copy.12.live, s32[1]{0:T(128)} %bitcast.me, f32[2,128,1024]{2,1,0:T(8,128)S(1)} %copy-done.1, f32[2,256,1024]{2,1,0:T(8,128)S(1)} %copy-done, ...), custom_call_target="tpu_custom_call" | custom-call | tf_op jit(solution)/shard_map/pallas_call | solution.py:240
  47.1 95.3 %shard_map.97 = (f32[2,256,512]{2,1,0:T(8,128)S(1)}, f32[2,4,256,256]{3,2,1,0:T(8,128)S(1)}) custom-call(f32[2,512,1024]{2,1,0:T(8,128)} %get-tuple-element.10.grad, f32[2,8,256,256]{3,2,1,0:T(8,128)} %get-tuple-element.11.pgrad), custom_call_target="tpu_custom_call" | custom-call | tf_op jit(solution)/shard_map/pallas_call | solution.py:489
  142.5 1.0 copy.13
  143.5 1.3 copy.14
Async XLA Ops:
  1.3 29.1 %copy-start = (f32[2,256,1024]{2,1,0:T(8,128)S(1)}, f32[2,256,1024]{2,1,0:T(8,128)}, u32[]{:S(2)}) copy-start(f32[2,256,1024]{2,1,0:T(8,128)} %obj.3) | copy-start | bytes 6291460
  1.3 29.1 %copy-start.3 = (bf16[512,512]{1,0:T(8,128)(2,1)S(1)}, bf16[512,512]{1,0:T(8,128)(2,1)}, u32[]{:S(2)}) copy-start(bf16[512,512]{1,0:T(8,128)(2,1)} %constant.9.clone.right) | copy-start | bytes 1572868
  1.3 29.1 %copy-start.4 = (bf16[512,512]{1,0:T(8,128)(2,1)S(1)}, bf16[512,512]{1,0:T(8,128)(2,1)}, u32[]{:S(2)}) copy-start(bf16[512,512]{1,0:T(8,128)(2,1)} %constant.8.clone.left) | copy-start | bytes 1572868
  1.3 29.1 %copy-start.5 = (s32[8]{0:T(128)S(1)}, s32[8]{0:T(128)}, u32[]{:S(2)}) copy-start(s32[8]{0:T(128)} %rows.1) | copy-start | bytes 100
  1.3 29.1 %copy-start.6 = (s32[8]{0:T(128)S(1)}, s32[8]{0:T(128)}, u32[]{:S(2)}) copy-start(s32[8]{0:T(128)} %cols.1) | copy-start | bytes 100
  30.5 1.2 copy-start.1
  31.7 1.2 copy-start.2

commit v3 on v2

--- a/solution.py
+++ b/solution.py
@@ -156,6 +156,16 @@
         copy.wait()
     count = (live[0] - m + peers - 1) // peers
 
+    batch, groups = 2, modes // 2
+
+    def twice(rows_table, wave, cols_table):
+        halfp = jnp.dot(rows_table, wave, preferred_element_type=F32).astype(BF16)
+        parts = [
+            jnp.concatenate([halfp[:win, k * win:(k + 1) * win], halfp[win:, k * win:(k + 1) * win]], axis=1)
+            for k in range(batch)
+        ]
+        return [jnp.dot(part, cols_table, preferred_element_type=F32) for part in parts]
+
     def position(i, carry):
         slot = m + i * peers
         fetch = pltpu.make_async_copy(measured.at[slot], meas.at[0], sems.at[3])
@@ -174,54 +184,54 @@
             patch[part] = pltpu.roll(block, (wide - shift) % wide, 1)[:, :win]
         meas[1] = jnp.zeros((win, win), F32)
 
-        def forward(pair, carry):
-            pr, pi = patch[0], patch[1]
-            exits = []
-            for k in range(2):
-                qr, qi = prb[0, 2 * pair + k], prb[1, 2 * pair + k]
-                er = (qr * pr - qi * pi).astype(BF16)
-                ei = (qr * pi + qi * pr).astype(BF16)
-                exits.append(jnp.concatenate([er, ei], axis=0))
-            wave = jnp.concatenate(exits, axis=1)
-            halfp = jnp.dot(left[...], wave, preferred_element_type=F32).astype(BF16)
-            for k in range(2):
-                lhs = jnp.concatenate(
-                    [halfp[:win, k * win:(k + 1) * win], halfp[win:, k * win:(k + 1) * win]], axis=1)
-                out = jnp.dot(lhs, right[...], preferred_element_type=F32)
-                far[2 * pair + k] = out
-                fr, fi = out[:, :win], out[:, win:]
-                meas[1] += fr * fr + fi * fi
+        def forward(step, carry):
+            for g in range(groups):
+                first = (step * groups + g) * batch
+                pr, pi = patch[0], patch[1]
+                exits = []
+                for k in range(batch):
+                    qr, qi = prb[0, first + k], prb[1, first + k]
+                    er = (qr * pr - qi * pi).astype(BF16)
+                    ei = (qr * pi + qi * pr).astype(BF16)
+                    exits.append(jnp.concatenate([er, ei], axis=0))
+                outs = twice(left[...], jnp.concatenate(exits, axis=1), right[...])
+                total = meas[1]
+                for k in range(batch):
+                    far[first + k] = outs[k]
+                    fr, fi = outs[k][:, :win], outs[k][:, win:]
+                    total += fr * fr + fi * fi
+                meas[1] = total
             return carry
 
-        lax.fori_loop(0, modes // 2, forward, 0)
+        lax.fori_loop(0, modes // (batch * groups), forward, 0)
         fetch.wait()
         meas[1] = 1.0 - jnp.sqrt(meas[0]) / jnp.maximum(jnp.sqrt(meas[1]), 0.5)
         terms[...] = jnp.zeros(terms.shape, F32)
 
-        def backward(pair, carry):
-            scaling = meas[1]
-            chis = []
-            for k in range(2):
-                value = far[2 * pair + k]
-                chis.append(jnp.concatenate(
-                    [(value[:, :win] * scaling).astype(BF16), (value[:, win:] * scaling).astype(BF16)], axis=0))
-            wave = jnp.concatenate(chis, axis=1)
-            halfp = jnp.dot(right[...], wave, preferred_element_type=F32).astype(BF16)
-            for k in range(2):
-                mode = 2 * pair + k
-                lhs = jnp.concatenate(
-                    [halfp[:win, k * win:(k + 1) * win], halfp[win:, k * win:(k + 1) * win]], axis=1)
-                back = jnp.dot(lhs, left[...], preferred_element_type=F32)
-                br, bi = back[:, :win], back[:, win:]
+        def backward(step, carry):
+            for g in range(groups):
+                first = (step * groups + g) * batch
+                scaling = meas[1]
+                chis = []
+                for k in range(batch):
+                    value = far[first + k]
+                    chis.append(jnp.concatenate(
+                        [(value[:, :win] * scaling).astype(BF16), (value[:, win:] * scaling).astype(BF16)], axis=0))
+                outs = twice(right[...], jnp.concatenate(chis, axis=1), left[...])
                 pr, pi = patch[0], patch[1]
-                qr, qi = prb[0, mode], prb[1, mode]
-                terms[0, :win, :win] += qr * br + qi * bi
-                terms[1, :win, :win] += qr * bi - qi * br
-                pgrad[0, mode] += pr * br + pi * bi
-                pgrad[1, mode] += pr * bi - pi * br
+                tr, ti = terms[0, :win, :win], terms[1, :win, :win]
+                for k in range(batch):
+                    br, bi = outs[k][:, :win], outs[k][:, win:]
+                    qr, qi = prb[0, first + k], prb[1, first + k]
+                    tr += qr * br + qi * bi
+                    ti += qr * bi - qi * br
+                    pgrad[0, first + k] += pr * br + pi * bi
+                    pgrad[1, first + k] += pr * bi - pi * br
+                terms[0, :win, :win] = tr
+                terms[1, :win, :win] = ti
             return carry
 
-        lax.fori_loop(0, modes // 2, backward, 0)
+        lax.fori_loop(0, modes // (batch * groups), backward, 0)
         for part in range(2):
             grad[part, pl.ds(top, tall), pl.ds(base, wide)] += pltpu.roll(pltpu.roll(terms[part], shift, 1), drop, 0)
         return carry
@@ -260,7 +270,7 @@
 
 
 def reduce_kernel(tiles, peers, half, grad, pgrad, ograd, oprobe,
-                  edge, sibp, modep, mine, nearp, farp, objp,
+                  inner, ours, edge, sibp, modep, mine, nearp, farp, objp, load,
                   edge_s, edge_r, sib_s, sib_r, mode_s, mode_r, near_s, near_r, far_s, far_r,
                   obj_s, obj_r, back_near_s, back_near_r, back_far_s, back_far_r, fw_s, fw_r):
     t = lax.axis_index("tile")
@@ -300,6 +310,9 @@
     hello(near, m)
     pl.semaphore_wait(barrier, peers + highs - 1 + (t + tiles - 1) // tiles + (2 * tiles - 2 - t) // tiles)
 
+    fetch_inner = pltpu.make_async_copy(grad.at[:, pl.ds(half, tile_rows)], inner, load.at[0])
+    fetch_ours = pltpu.make_async_copy(pgrad.at[:, :, pl.ds(c * hw, hw)], ours, load.at[1])
+
     def remote(src, dst, ssem, rsem, tt, mm):
         return pltpu.make_async_remote_copy(
             src_ref=src, dst_ref=dst, send_sem=ssem, recv_sem=rsem,
@@ -320,7 +333,7 @@
     def obj_copy(d, upper):
         column = ((m + d) % peers) * width
         hr = tile_rows // 2
-        return remote(grad.at[:, pl.ds(half + upper * hr, hr), pl.ds(column, width)],
+        return remote(inner.at[:, pl.ds(upper * hr, hr), pl.ds(column, width)],
                       objp.at[d - 1, :, pl.ds(upper * hr, hr)],
                       obj_s.at[d - 1, upper], obj_r.at[d - 1, upper], t, (m + d) % peers)
 
@@ -388,15 +401,19 @@
     def _():
         to_prev.start()
 
+    fetch_ours.start()
+    fetch_inner.start()
+    fetch_ours.wait()
     for part in range(2):
         for d in range(1, peers):
             group = ((m + d) % peers) * nm
             sib_copy(d, part).wait_recv()
-            sibp[d, part] += pgrad[part, pl.ds(group, nm), pl.ds(c * hw, hw)]
+            sibp[d, part] += ours[part, pl.ds(group, nm)]
             mode_copy(d, part).start()
     for part in range(2):
         sib_copy(0, part).wait_recv()
-        mine[part] = sibp[0, part] + pgrad[part, pl.ds(m * nm, nm), pl.ds(c * hw, hw)]
+        mine[part] = sibp[0, part] + ours[part, pl.ds(m * nm, nm)]
+    fetch_inner.wait()
 
     for d in range(1, peers):
         mode_copy(d, 0).wait_recv()
@@ -406,7 +423,7 @@
     @pl.when(t > 0)
     def _():
         to_next.wait_recv()
-        grad[:, pl.ds(half, half)] += edge[0]
+        inner[:, pl.ds(0, half)] += edge[0]
 
     for d in range(1, peers):
         obj_copy(d, 0).start()
@@ -414,7 +431,7 @@
     @pl.when(t < tiles - 1)
     def _():
         to_prev.wait_recv()
-        grad[:, pl.ds(tile_rows, half)] += edge[1]
+        inner[:, pl.ds(tile_rows - half, half)] += edge[1]
 
     for d in range(1, peers):
         obj_copy(d, 1).start()
@@ -442,7 +459,7 @@
     for d in range(1, highs):
         back_far(1, d).start()
 
-    ograd[...] = grad[:, pl.ds(half, tile_rows), pl.ds(pl.multiple_of(m * width, 128), width)]
+    ograd[...] = inner[:, :, pl.ds(pl.multiple_of(m * width, 128), width)]
     back_near(0).wait_recv()
     fw_copy(0).start()
     for d in range(1, highs):
@@ -486,15 +503,18 @@
     width = cols // peers
     dma = pltpu.SemaphoreType.DMA
     vmem = pl.BlockSpec(memory_space=pltpu.VMEM)
+    anyspace = pl.BlockSpec(memory_space=pl.ANY)
     return pl.pallas_call(
         functools.partial(reduce_kernel, tiles, peers, half),
         out_shape=(
             jax.ShapeDtypeStruct((2, tile_rows, width), F32),
             jax.ShapeDtypeStruct((2, nm, win, win), F32),
         ),
-        in_specs=[vmem, vmem],
+        in_specs=[anyspace, anyspace],
         out_specs=(vmem, vmem),
         scratch_shapes=[
+            pltpu.VMEM((2, tile_rows, cols), F32),
+            pltpu.VMEM((2, modes, hw, win), F32),
             pltpu.VMEM((2, 2, half, cols), F32),
             pltpu.VMEM((peers, 2, nm, hw, win), F32),
             pltpu.VMEM((peers - 1, 2, nm, hw, win), F32),
@@ -502,7 +522,7 @@
             pltpu.VMEM((2, nm, hw // 2, win), F32),
             pltpu.VMEM((2, highs - 1, nm, hw // highs, win), F32),
             pltpu.VMEM((peers - 1, 2, tile_rows, width), F32),
-            dma((2,)), dma((2,)), dma((peers, 2)), dma((peers, 2)), dma((peers - 1, 2)), dma((peers - 1, 2)),
+            dma((2,)), dma((2,)), dma((2,)), dma((peers, 2)), dma((peers, 2)), dma((peers - 1, 2)), dma((peers - 1, 2)),
             dma((2,)), dma((2,)), dma((2, highs - 1)), dma((2, highs - 1)),
             dma((peers - 1, 2)), dma((peers - 1, 2)),
             dma((2,)), dma((2,)), dma((2, highs - 1)), dma((2, highs - 1)), dma((2,)), dma((2,)),

time: 145 us -> 137 us (0.945)
  Pallas kernels: 139 us -> 130 us
    pallas_call x1, Pallas kernels: 95.3 us -> 69.4 us  [reduce(): pl.pallas_call(functools.partial(reduce_kernel, tiles, peers, half), out_...]
    pallas_call x1, Pallas kernels: 14.2 us -> 31.8 us  [compute(): pl.pallas_call(functools.partial(compute_kernel, half, peers), out_shape=...]
where the time goes in v3:
time: 137 us; the launch traced here: 136 us
  Pallas kernels  130 us (95%)
  local copies, waits for them, and re-layouts  4.76 us (3%)
  between operations  1.39 us (1%)
    pallas_call x1, Pallas kernels, reduce(): pl.pallas_call(functools.partial(reduce_kernel, tiles, peers, half), out_...  69.4 us
    pallas_call x1, Pallas kernels, compute(): pl.pallas_call(functools.partial(compute_kernel, half, peers), out_shape=...  31.8 us
    pallas_call x1, Pallas kernels, gather(): pl.pallas_call(functools.partial(gather_kernel, tiles, peers, half), out_...  29.1 us
    unnamed x16, local copies, waits for them, and re-layouts  4.76 us

profile of v3, /device:TPU:0, one launch (start us, length us, event | category | flops | bytes accessed | tf_op | source)
XLA Modules:
  0.0 136.3 jit_solution(11800117981655523745)
XLA Ops:
  1.3 0.0 copy-start
  1.3 0.0 copy-start.3
  1.3 0.0 copy-start.4
  1.3 0.0 copy-start.5
  1.3 0.0 copy-start.6
  1.3 29.1 %shard_map.95 = (f32[2,128,1024]{2,1,0:T(8,128)}, f32[2,128,1024]{2,1,0:T(8,128)}, f32[2,8,256,256]{3,2,1,0:T(8,128)}) custom-call(f32[2,256,1024]{2,1,0:T(8,128)} %obj.3, f32[2,4,256,256]{3,2,1,0:T(8,128)} %own.1), custom_call_target="tpu_custom_call" | custom-call | tf_op jit(solution)/shard_map/pallas_call | solution.py:120
  30.4 0.0 copy-done
  30.4 0.0 copy-done.3
  30.4 0.0 copy-done.4
  30.4 0.0 copy-done.5
  30.4 0.0 copy-done.6
  30.5 0.0 copy-start.1
  30.5 1.2 copy-done.1
  31.7 0.0 copy-start.2
  31.7 1.2 copy-done.2
  32.9 31.8 %shard_map.96 = (f32[2,512,1024]{2,1,0:T(8,128)}, f32[2,8,256,256]{3,2,1,0:T(8,128)}) custom-call(s32[8]{0:T(128)S(1)} %copy-done.5, s32[8]{0:T(128)S(1)} %copy-done.6, s32[1]{0:T(128)S(6)} %copy.12.live, s32[1]{0:T(128)} %bitcast.me, f32[2,128,1024]{2,1,0:T(8,128)S(1)} %copy-done.1, f32[2,256,1024]{2,1,0:T(8,128)S(1)} %copy-done, ...), custom_call_target="tpu_custom_call" | custom-call | tf_op jit(solution)/shard_map/pallas_call | solution.py:250
  64.7 69.4 %shard_map.97 = (f32[2,256,512]{2,1,0:T(8,128)S(1)}, f32[2,4,256,256]{3,2,1,0:T(8,128)S(1)}) custom-call(f32[2,512,1024]{2,1,0:T(8,128)} %get-tuple-element.10.grad, f32[2,8,256,256]{3,2,1,0:T(8,128)} %get-tuple-element.11.pgrad), custom_call_target="tpu_custom_call" | custom-call | tf_op jit(solution)/shard_map/pallas_call | solution.py:507
  134.0 1.0 copy.13
  135.0 1.3 copy.14
Async XLA Ops:
  1.3 29.1 %copy-start = (f32[2,256,1024]{2,1,0:T(8,128)S(1)}, f32[2,256,1024]{2,1,0:T(8,128)}, u32[]{:S(2)}) copy-start(f32[2,256,1024]{2,1,0:T(8,128)} %obj.3) | copy-start | bytes 6291460
  1.3 29.1 %copy-start.3 = (bf16[512,512]{1,0:T(8,128)(2,1)S(1)}, bf16[512,512]{1,0:T(8,128)(2,1)}, u32[]{:S(2)}) copy-start(bf16[512,512]{1,0:T(8,128)(2,1)} %constant.9.clone.right) | copy-start | bytes 1572868
  1.3 29.1 %copy-start.4 = (bf16[512,512]{1,0:T(8,128)(2,1)S(1)}, bf16[512,512]{1,0:T(8,128)(2,1)}, u32[]{:S(2)}) copy-start(bf16[512,512]{1,0:T(8,128)(2,1)} %constant.8.clone.left) | copy-start | bytes 1572868
  1.3 29.1 %copy-start.5 = (s32[8]{0:T(128)S(1)}, s32[8]{0:T(128)}, u32[]{:S(2)}) copy-start(s32[8]{0:T(128)} %rows.1) | copy-start | bytes 100
  1.3 29.1 %copy-start.6 = (s32[8]{0:T(128)S(1)}, s32[8]{0:T(128)}, u32[]{:S(2)}) copy-start(s32[8]{0:T(128)} %cols.1) | copy-start | bytes 100
  30.5 1.2 copy-start.1
  31.7 1.2 copy-start.2
